TPU v7x, 128 devices: a whole 4x4x4 slice. The times are simulated.
128 devices in a mesh: grp: 16 (over y, z), tp: 8 (over x, core).
Axes of the slice: x: 4, y: 4, z: 4, core: 2. Of those that a mesh axis runs over, the one named last changes fastest.
Arguments:
- queries: bfloat16 [32, 8192], P(None, 'tp'), may hold values from -9 to 9, as said below
- cache_keys: bfloat16 [32, 16384, 1024], P(None, 'grp', 'tp'), may hold values from -6 to 6
- cache_values: bfloat16 [32, 16384, 1024], P(None, 'grp', 'tp'), may hold values from -6 to 6
- lengths: int32 [32], replicated, may hold values from 4096 to 16384, as said below
- new_keys: bfloat16 [16384, 1024], P('grp', 'tp'), may hold values from -6 to 6
- new_values: bfloat16 [16384, 1024], P('grp', 'tp'), may hold values from -6 to 6
- new_rows: int32 [16384], P('grp'), may hold values from 0 to 31
- owners: int32 [16384, 1], P('grp'), may hold values from 0 to 15; in each aligned block of 1024 rows (0 to 1023, 1024 to 2047, ...) at most 128 rows name the same one
- out_weight: bfloat16 [8192, 8192], P('tp', 'grp'), may hold values from -0.0625 to 0.0625
Outputs:
- mixed: bfloat16 [32, 8192], P(None, ('grp', 'tp'))
- pool_kv: bfloat16 [2, 32768, 1024], P(None, 'grp', 'tp')
Inputs may be any that keep to these rules, and one draw needn't show every extreme that they name: In the hidden draw some queries may be far larger than typical ones. `lengths`: some sequence is exactly 16384 long. `owners`: within each aligned block of 1024 fresh tokens (those of one grp index) at most 128 name the same owner, a bound that some block reaches.
All inputs are finite; a program needn't handle non-finite values.
Results may differ from a plain program's by a relative error of at most 0.0048.
Values may be sent and summed in bfloat16 or wider, within the bound.
A program may use at most 64 MiB of HBM per device.

v0:
```python
import jax
import jax.numpy as jnp
from jax import lax
from jax.sharding import PartitionSpec as P

HEADS = 64
KV_HEADS = 8
HEAD_DIM = 128


NEG = -1e30


def combined_all(part, axis, combine):
    gathered = jax.tree.map(lambda a: lax.all_gather(a, axis), part)

    def take(source):
        return jax.tree.map(lambda a: lax.dynamic_index_in_dim(a, source, 0, False), gathered)

    return lax.fori_loop(
        1, lax.axis_size(axis), lambda source, state: combine(state, take(source)), take(0)
    )


def finish_partial(scores, allowed, values, form):
    scores = jnp.where(allowed, scores, NEG)
    highest = jnp.max(scores, axis=-1)
    weights = jnp.where(allowed, jnp.exp(scores - highest[..., None]), 0.0)
    total = jnp.sum(weights, axis=-1)
    summed = jnp.einsum(
        form,
        weights,
        values.astype(jnp.float32),
        precision=lax.Precision.HIGHEST,
        preferred_element_type=jnp.float32,
    )
    return (highest, total, summed)


def attend_cache(query_heads, keys, values, allowed):
    scores = jnp.einsum(
        "bkgd,btkd->bkgt", query_heads, keys, preferred_element_type=jnp.float32
    ) * HEAD_DIM ** (-0.5)
    return finish_partial(scores, allowed[:, None, None, :], values, "bkgt,btkd->bkgd")


def attend_fresh(query_heads, keys, values, owner_rows, row_count):
    scores = jnp.einsum(
        "bkgd,tkd->bkgt", query_heads, keys, preferred_element_type=jnp.float32
    ) * HEAD_DIM ** (-0.5)
    allowed = owner_rows[None, :] == jnp.arange(row_count, dtype=jnp.int32)[:, None]
    return finish_partial(scores, allowed[:, None, None, :], values, "bkgt,tkd->bkgd")


def join_partials(first, second):
    high_a, total_a, summed_a = first
    high_b, total_b, summed_b = second
    highest = jnp.maximum(high_a, high_b)
    factor_a = jnp.exp(high_a - highest)
    factor_b = jnp.exp(high_b - highest)
    return (
        highest,
        total_a * factor_a + total_b * factor_b,
        summed_a * factor_a[..., None] + summed_b * factor_b[..., None],
    )


def on_device(
    queries, cache_keys, cache_values, lengths, new_keys, new_values, new_rows, owners, out_weight
):
    row_count = queries.shape[0]
    kv_width = cache_keys.shape[2]
    kv_local = kv_width // HEAD_DIM
    group_size = HEADS // KV_HEADS
    seq_local = cache_keys.shape[1]
    fresh_count = new_keys.shape[0]
    indices = lax.axis_size("grp")
    capacity = 2 * fresh_count // indices
    query_heads = queries.reshape(row_count, kv_local, group_size, HEAD_DIM)
    positions = lax.axis_index("grp") * seq_local + jnp.arange(seq_local, dtype=jnp.int32)
    allowed = positions[None, :] < lengths[:, None]
    cache_part = attend_cache(
        query_heads,
        cache_keys.reshape(row_count, seq_local, kv_local, HEAD_DIM),
        cache_values.reshape(row_count, seq_local, kv_local, HEAD_DIM),
        allowed,
    )
    destination = owners[:, 0]
    onehot = (destination[:, None] == jnp.arange(indices, dtype=jnp.int32)[None, :]).astype(
        jnp.int32
    )
    rank = jnp.sum((jnp.cumsum(onehot, axis=0) - onehot) * onehot, axis=1)
    slot_index = destination * capacity + rank
    placing = slot_index[None, :] == jnp.arange(indices * capacity, dtype=jnp.int32)[:, None]
    stacked = jnp.concatenate([new_keys, new_values], axis=1)
    outgoing = jnp.dot(placing.astype(jnp.bfloat16), stacked, preferred_element_type=jnp.float32)
    outgoing = outgoing.astype(jnp.bfloat16).reshape(indices, capacity, 2 * kv_width)
    outgoing_rows = jnp.max(jnp.where(placing, new_rows[None, :], -1), axis=1).reshape(
        indices, capacity
    )
    arrived, arrived_rows = (
        lax.all_to_all(outgoing, "grp", split_axis=0, concat_axis=0, tiled=True),
        lax.all_to_all(outgoing_rows, "grp", split_axis=0, concat_axis=0, tiled=True),
    )
    arrived = arrived.reshape(indices * capacity, 2 * kv_width)
    pool_kv = jnp.stack([arrived[:, :kv_width], arrived[:, kv_width:]])
    fresh_part = attend_fresh(
        query_heads,
        arrived[:, :kv_width].reshape(indices * capacity, kv_local, HEAD_DIM),
        arrived[:, kv_width:].reshape(indices * capacity, kv_local, HEAD_DIM),
        arrived_rows.reshape(indices * capacity),
        row_count,
    )
    local_part = join_partials(cache_part, fresh_part)
    highest, total, summed = combined_all(local_part, "grp", join_partials)
    attended = (
        (summed / total[..., None]).reshape(row_count, kv_width * group_size).astype(jnp.bfloat16)
    )
    term = jnp.dot(attended, out_weight, preferred_element_type=jnp.float32)
    mixed = lax.psum_scatter(term, "tp", scatter_dimension=1, tiled=True).astype(jnp.bfloat16)
    return (mixed, pool_kv)


def solution(mesh):
    placed = (
        P(None, "tp"),
        P(None, "grp", "tp"),
        P(None, "grp", "tp"),
        P(),
        P("grp", "tp"),
        P("grp", "tp"),
        P("grp"),
        P("grp", None),
        P("tp", "grp"),
    )
    return jax.shard_map(
        on_device,
        mesh=mesh,
        in_specs=placed,
        out_specs=(P(None, ("grp", "tp")), P(None, "grp", "tp")),
        check_vma=False,
    )
```

profile of v0, /device:TPU:1, one launch (start us, length us, event | category | flops | bytes accessed | tf_op | source)
XLA Modules:
  0.0 167.4 jit_solution(14002294430364336887)
XLA Ops:
  7.2 0.8 fusion.49
  8.0 4.5 %reduce-window.6 = s32[16,8,128]{2,1,0:T(8,128)S(1)} reduce-window(s32[16,8,128]{2,1,0:T(8,128)S(1)} %fusion.49, s32[]{:T(128)} %constant.69.clone.1), window={size=1x1x128 pad=0_0x0_0x127_0}, to_apply=%region_1.2 | reduce-window | flops 2080768 | bytes 131076 | tf_op jit(solution)/shard_map/reduce-window
  12.5 0.1 slice.22
  12.5 0.1 copy.67
  12.8 0.1 broadcast_add_fusion
  12.9 0.7 fusion.46
  13.6 0.7 multiply_add_fusion
  14.3 2.5 %select_reduce_fusion = s32[2048]{0:T(1024)} fusion(s32[1024]{0:T(1024)} %param.17, s32[1024]{0:T(1024)S(1)} %multiply_add_fusion), kind=kLoop, calls=%fused_computation.10 | loop fusion | flops 6289408 | bytes 16384 | tf_op jit(solution)/shard_map/reduce_max | solution.py:98
  16.8 8.6 %all-to-all-start = ((s32[16,1,128]{2,1,0:T(1,128)}), s32[16,1,128]{2,1,0:T(1,128)S(1)}, u32[]{:S(2)}, u32[]{:S(2)}) async-start(s32[16,1,128]{2,1,0:T(1,128)} %bitcast.10), calls=%async_computation | async-start | bytes 16384 | tf_op jit(solution)/shard_map/all_to_all | solution.py:103
  25.4 3.6 %fusion.8 = bf16[2048,256]{1,0:T(8,128)(2,1)} fusion(s32[1024]{0:T(1024)S(1)} %multiply_add_fusion, bf16[1024,128]{1,0:T(8,128)(2,1)} %param.16, bf16[1024,128]{1,0:T(8,128)(2,1)} %param.15), kind=kOutput, calls=%fused_computation.16 | convolution fusion | flops 1077411840 | bytes 1576960 | tf_op jit(solution)/shard_map/dot_general | solution.py:96
  29.0 2.7 %all-to-all-done = s32[16,1,128]{2,1,0:T(1,128)S(1)} async-done(((s32[16,1,128]{2,1,0:T(1,128)}), s32[16,1,128]{2,1,0:T(1,128)S(1)}, u32[]{:S(2)}, u32[]{:S(2)}) %all-to-all-start) | async-done | bytes 8224 | tf_op jit(solution)/shard_map/all_to_all | solution.py:103
  31.7 4.1 %all-to-all-start.1 = ((bf16[16,128,256]{2,1,0:T(8,128)(2,1)}), bf16[16,128,256]{2,1,0:T(8,128)(2,1)S(1)}, u32[]{:S(2)}, u32[]{:S(2)}) async-start(bf16[16,128,256]{2,1,0:T(8,128)(2,1)} %bitcast.12), calls=%async_computation.1 | async-start | bytes 2097152 | tf_op jit(solution)/shard_map/all_to_all | solution.py:102
  35.9 0.1 broadcast_compare_fusion
  36.0 5.7 %fusion.58 = (f32[32,8]{1,0:T(8,128)S(1)}, f32[32,8,1024]{2,1,0:T(8,128)S(1)}) fusion(bf16[32,8,128]{2,1,0:T(8,128)(2,1)S(1)} %bitcast.155, bf16[32,1024,128]{2,1,0:T(8,128)(2,1)} %param.12, pred[32,1024]{1,0:T(8,128)(4,1)S(1)} %broadcast_compare_fusion), kind=kOutput, calls=%fused_computation.82 | convolution fusion | flops 67895040 | bytes 9536512 | tf_op jit(solution)/shard_map/bkgd,btkd->bkgt/dot_general | solution.py:41
  41.9 9.2 %all-to-all-done.1 = bf16[16,128,256]{2,1,0:T(8,128)(2,1)S(1)} async-done(((bf16[16,128,256]{2,1,0:T(8,128)(2,1)}), bf16[16,128,256]{2,1,0:T(8,128)(2,1)S(1)}, u32[]{:S(2)}, u32[]{:S(2)}) %all-to-all-start.1) | async-done | bytes 1048608 | tf_op jit(solution)/shard_map/all_to_all | solution.py:102
  51.0 0.6 fusion.57
  51.6 1.8 %fusion.12 = (f32[32,8,2048]{2,0,1:T(8,128)}, f32[32,8]{0,1:T(8,128)S(1)}) fusion(f32[32,1,8,2048]{3,0,2,1:T(8,128)S(1)} %get-tuple-element.243, f32[32,8]{0,1:T(8,128)S(1)} %get-tuple-element.242, pred[32,2048]{1,0:T(8,128)(4,1)S(1)} %iota_compare_fusion.4), kind=kLoop, calls=%fused_computation.21 | loop fusion | flops 1572608 | bytes 4261888 | tf_op jit(solution)/shard_map/reshape.31
  53.4 0.1 copy.76
  53.5 6.0 %fusion.30 = f32[32,1,8,128]{3,2,0,1:T(8,128)S(1)} fusion(bf16[32,1024,128]{2,1,0:T(8,128)(2,1)} %param.13, f32[32,8,1024]{2,1,0:T(8,128)S(1)} %get-tuple-element.245, f32[32,8]{1,0:T(8,128)S(1)} %get-tuple-element.244, pred[32,1024]{1,0:T(8,128)(4,1)S(1)} %broadcast_compare_fusion, f32[32,8]{1,0:T(8,128)S(1)} %copy.76), kind=kOutput, calls=%fused_computation.32 | convolution fusion | flops 403210240 | bytes 9603072 | tf_op jit(solution)/shard_map/bkgt,btkd->bkgd/dot_general | solution.py:30
  59.6 3.0 %fusion.27 = f32[32,1,8,128]{3,2,1,0:T(8,128)} fusion(f32[32,1,8,128]{3,2,0,1:T(8,128)S(1)} %fusion.30, f32[32,8,2048]{2,0,1:T(8,128)S(1)} %copy-done.1, bf16[2048,256]{1,0:T(8,128)(2,1)S(1)} %bitcast.152, f32[32,8]{1,0:T(8,128)S(1)} %copy.78), kind=kOutput, calls=%fused_computation.30 | convolution fusion | flops 805371904 | bytes 2899968 | tf_op jit(solution)/shard_map/bkgt,tkd->bkgd/dot_general | solution.py:30
  62.6 0.4 fusion.31
  63.3 17.0 %all_gather.15 = f32[16,32,1,8]{1,3,2,0:T(8,128)S(1)} all-gather(f32[1,32,1,8]{1,3,2,0:T(8,128)S(1)} %copy.73), channel_id=1, replica_groups=mesh['grp'=16,'tp'=8] {'grp'}, dimensions={0}, use_global_device_ids=true | all-gather | bytes 17408 | tf_op jit(solution)/shard_map/all_gather | solution.py:15
  80.3 17.2 %all_gather.14 = f32[16,32,1,8]{1,3,2,0:T(8,128)S(1)} all-gather(f32[1,32,1,8]{1,3,2,0:T(8,128)S(1)} %copy.71), channel_id=1, replica_groups=mesh['grp'=16,'tp'=8] {'grp'}, dimensions={0}, use_global_device_ids=true | all-gather | bytes 17408 | tf_op jit(solution)/shard_map/all_gather | solution.py:15
  97.5 0.9 slice_bitcast_fusion.1
  98.4 8.6 %all-gather.3.cloned.1.call-done = f32[512,1,8,128]{3,2,1,0:T(8,128)} async-done(((f32[32,1,8,128]{3,2,1,0:T(8,128)}), f32[512,1,8,128]{3,2,1,0:T(8,128)}) %all-gather.3.cloned.1.call-update) | async-done | bytes 2097168 | tf_op jit(solution)/shard_map/all_gather | solution.py:15
  107.0 0.9 slice.26
  107.9 19.4 %while.19 = (s32[]{:T(128)}, f32[32,1,8]{0,2,1:T(8,128)S(1)}, f32[32,1,8]{0,2,1:T(8,128)S(1)}, f32[32,1,8,128]{3,2,1,0:T(8,128)S(1)}, f32[16,32,1,8]{1,3,2,0:T(8...) while((s32[]{:T(128)}, f32[32,1,8]{0,2,1:T(8,128)S(1)}, ...), condition=%wide.region_9.10_spmd, body=%wide.region_8.9_spmd.sunk | while | flops 100101 | bytes 412827 | solution.py:20
  108.0 0.1 copy.115
  108.1 1.1 fusion.69
  109.4 1.1 fusion.69
  110.7 1.1 fusion.69
  112.0 1.1 fusion.69
  113.3 1.1 fusion.69
  114.6 1.1 fusion.69
  115.9 1.1 fusion.69
  117.2 1.1 fusion.69
  118.5 1.1 fusion.69
  119.8 1.1 fusion.69
  121.1 1.1 fusion.69
  122.4 1.1 fusion.69
  123.7 1.1 fusion.69
  125.0 1.1 fusion.69
  126.2 1.1 fusion.69
  127.4 0.1 divide_convert_fusion
  127.5 1.2 convolution_bitcast_fusion
  128.8 1.1 pad_maximum_fusion
  129.9 29.3 %reduce-scatter.4.cloned.1.call-done = f32[64,32]{1,0:T(8,128)} async-done(((f32[512,32]{1,0:T(8,128)}), f32[64,32]{1,0:T(8,128)}) %reduce-scatter.4.cloned.1.call-update) | async-done | bytes 8208
  159.1 1.4 copy.85
  (105 shorter events, 3.5 us)
Async XLA Ops:
  7.2 120.4 %copy-start = (bf16[1024,512]{1,0:T(8,128)(2,1)S(1)}, bf16[1024,512]{1,0:T(8,128)(2,1)}, u32[]{:S(2)}) copy-start(bf16[1024,512]{1,0:T(8,128)(2,1)} %param.19) | copy-start | bytes 3145732
  16.8 14.9 %all-to-all-start = ((s32[16,1,128]{2,1,0:T(1,128)}), s32[16,1,128]{2,1,0:T(1,128)S(1)}, u32[]{:S(2)}, u32[]{:S(2)}) async-start(s32[16,1,128]{2,1,0:T(1,128)} %bitcast.10), calls=%async_computation | async-start | bytes 16384 | tf_op jit(solution)/shard_map/all_to_all | solution.py:103
  29.0 6.9 %copy-start.4 = (s32[32]{0:T(128)S(1)}, s32[32]{0:T(128)}, u32[]{:S(2)}) copy-start(s32[32]{0:T(128)} %param.14) | copy-start | bytes 388
  29.0 7.0 %copy-start.3 = (bf16[32,1024]{1,0:T(8,128)(2,1)S(1)}, bf16[32,1024]{1,0:T(8,128)(2,1)}, u32[]{:S(2)}) copy-start(bf16[32,1024]{1,0:T(8,128)(2,1)} %param.11) | copy-start | bytes 196612
  31.7 19.3 %all-to-all-start.1 = ((bf16[16,128,256]{2,1,0:T(8,128)(2,1)}), bf16[16,128,256]{2,1,0:T(8,128)(2,1)S(1)}, u32[]{:S(2)}, u32[]{:S(2)}) async-start(bf16[16,128,256]{2,1,0:T(8,128)(2,1)} %bitcast.12), calls=%async_computation.1 | async-start | bytes 2097152 | tf_op jit(solution)/shard_map/all_to_all | solution.py:102
  35.8 71.2 %all-gather.3.cloned.1.call-start = ((), (), s32[]{:S(2)}) async-start(), calls=%async_computation.3 | async-start | bytes 2228224 | tf_op jit(solution)/shard_map/all_gather | solution.py:15
  53.5 6.0 %copy-start.1 = (f32[32,8,2048]{2,0,1:T(8,128)S(1)}, f32[32,8,2048]{2,0,1:T(8,128)}, u32[]{:S(2)}) copy-start(f32[32,8,2048]{2,0,1:T(8,128)} %get-tuple-element.234) | copy-start | bytes 6291460
  62.5 96.6 %reduce-scatter.4.cloned.1.call-start = ((), (), s32[]{:S(2)}) async-start(), calls=%async_computation.4 | async-start | bytes 294912
  107.9 20.9 %copy-start.2 = (bf16[1,2048,128]{2,1,0:T(8,128)(2,1)S(1)}, bf16[1,2048,128]{2,1,0:T(8,128)(2,1)}, u32[]{:S(2)}) copy-start(bf16[1,2048,128]{2,1,0:T(8,128)(2,1)} %get-tuple-element.237) | copy-start | bytes 1572868
Sparse Core Ops, SparseCore 0:
  62.7 44.2 all-gather.2
  128.9 30.1 reduce-scatter.3
where the time goes:
time: 170 us; the launch traced here: 167 us
  waiting for transfers between devices  49.8 us (29%)
  blocking collectives  34.2 us (20%)
  other arithmetic  29.2 us (17%)
  matrix products  20.1 us (12%)
  between operations  14.2 us (8%)
  starting transfers between devices  12.8 us (8%)
  local copies, waits for them, and re-layouts  6.42 us (4%)
    all_gather x2, blocking collectives, combined_all(): gathered = jax.tree.map(lambda a: lax.all_gather(a, axis), part)  34.2 us
    unnamed x3, waiting for transfers between devices  29.3 us
    add x15, other arithmetic, join_partials(): summed_a * factor_a[..., None] + summed_b * factor_b[..., None]  16 us
    all_to_all x1, waiting for transfers between devices, on_device(): lax.all_to_all(outgoing, 'grp', split_axis=0, concat_axis=0, tiled=True)  9.18 us
    dot_general x2, matrix products, finish_partial(): jnp.einsum(form, weights, values.astype(jnp.float32), precision=lax.Preci...  8.95 us
    all_gather x1, waiting for transfers between devices, combined_all(): gathered = jax.tree.map(lambda a: lax.all_gather(a, axis), part)  8.61 us
    all_to_all x1, starting transfers between devices, on_device(): lax.all_to_all(outgoing_rows, 'grp', split_axis=0, concat_axis=0, tiled=T...  8.6 us
    another operation x4, other arithmetic  6.4 us
  transfers between devices with their start and end apart: 4, of which 4 were waited for; matrix products, arithmetic and copies ran while one was open for 7% of the time, Pallas kernels for 0%

commit v1 on v0

v1 whole, which is shorter than its diff:
```python
import functools
import math

import jax
import jax.numpy as jnp
from jax import lax
from jax.experimental import pallas as pl
from jax.experimental.pallas import tpu as pltpu
from jax.sharding import PartitionSpec as P

MESH = pl.DeviceIdType.MESH
NT = (((1,), (1,)), ((), ()))
NN = (((1,), (0,)), ((), ()))
NEG = -1.0e30
FLOOR = -1.0e20
ROWS = 32
GROUP = 8
HEAD = 128
SEQ = 1024
FRESH = 1024
CAP = 128
BATCH = 4
F32 = jnp.float32
BF16 = jnp.bfloat16


def kernel(
    n,
    m,
    q_hbm, ck_hbm, cv_hbm, len_hbm, nk_hbm, nv_hbm, rows_hbm, own_hbm, w_hbm,
    mixed_ref, pool_ref,
    kb, vb, xb, wb, qin, qf, qb, lens, rowb, ownb,
    stage, sc, sf, pc, pf, acc, accf, stats, rs_out, rs_in, ag, tp_out, tp_in,
    in_sem, k_sem, v_sem, own_sem, big_s, big_r, st_s, st_r, rs_s, rs_r, ag_s, ag_r, tp_s, tp_r,
):
    g = lax.axis_index("grp")
    t = lax.axis_index("tp")
    scale = (HEAD**-0.5) * math.log2(math.e)
    steps = ROWS // BATCH
    chunk = ROWS * GROUP // n

    small = [
        pltpu.make_async_copy(own_hbm, ownb, in_sem.at[0]),
        pltpu.make_async_copy(nk_hbm, xb.at[:, pl.ds(0, HEAD)], in_sem.at[1]),
        pltpu.make_async_copy(nv_hbm, xb.at[:, pl.ds(HEAD, HEAD)], in_sem.at[2]),
        pltpu.make_async_copy(q_hbm, qin, in_sem.at[3]),
        pltpu.make_async_copy(rows_hbm, rowb, in_sem.at[4]),
        pltpu.make_async_copy(len_hbm, lens, in_sem.at[5]),
    ]
    weight = pltpu.make_async_copy(w_hbm, wb, in_sem.at[6])
    keys = [
        pltpu.make_async_copy(ck_hbm.at[pl.ds(c * BATCH, BATCH)], kb.at[pl.ds(c * BATCH, BATCH)], k_sem.at[c])
        for c in range(steps)
    ]
    values = [
        pltpu.make_async_copy(cv_hbm.at[pl.ds(c * BATCH, BATCH)], vb.at[pl.ds(c * BATCH, BATCH)], v_sem.at[c])
        for c in range(steps)
    ]
    for copy in small + keys:
        copy.start()

    barrier = pltpu.get_barrier_semaphore()
    for r in range(1, n):
        pl.semaphore_signal(barrier, inc=1, device_id=(lax.rem(g + r, n), t), device_id_type=MESH)
    for r in range(1, m):
        pl.semaphore_signal(barrier, inc=1, device_id=(g, lax.rem(t + r, m)), device_id_type=MESH)

    small[0].wait()
    own = ownb[...]
    blocks = FRESH // HEAD
    hot = jnp.concatenate([(own == o).astype(F32) for o in range(n)], axis=0).astype(BF16)
    ri = lax.broadcasted_iota(jnp.int32, (HEAD, HEAD), 0)
    ci = lax.broadcasted_iota(jnp.int32, (HEAD, HEAD), 1)
    before = (ri < ci).astype(F32).astype(BF16)
    ra = lax.broadcasted_iota(jnp.int32, (n * blocks, n * blocks), 0)
    ca = lax.broadcasted_iota(jnp.int32, (n * blocks, n * blocks), 1)
    upper = jnp.logical_and(ra // blocks == ca // blocks, ca < ra).astype(F32).astype(BF16)
    within = lax.dot_general(hot, before, NN, preferred_element_type=F32)
    ahead = lax.dot_general(upper, hot, NN, preferred_element_type=F32).astype(BF16)
    ahead = lax.dot_general(ahead, jnp.ones((HEAD, HEAD), BF16), NN, preferred_element_type=F32)
    counted = (within + ahead) * hot.astype(F32)
    rank = counted[0:blocks]
    for o in range(1, n):
        rank = rank + counted[o * blocks : (o + 1) * blocks]

    small[1].wait()
    small[2].wait()
    place = lax.broadcasted_iota(jnp.int32, (CAP, HEAD), 0).astype(F32).astype(BF16)
    big = [None] * n
    per = 4
    for part in range(n // per):
        lhs = []
        for r in range(part * per + 1, part * per + per + 1):
            d = lax.rem(g + r, n)
            named = jnp.where(own == d, rank, -1.0)
            columns = []
            for c in range(blocks):
                line = jnp.broadcast_to(named[c : c + 1, :], (CAP, HEAD)).astype(BF16)
                columns.append(jnp.where(line == place, jnp.bfloat16(1), jnp.bfloat16(0)))
            lhs.append(jnp.concatenate(columns, axis=1))
        placed = lax.dot_general(
            jnp.concatenate(lhs, axis=0), xb[...], NN, preferred_element_type=F32
        ).astype(BF16)
        for i in range(per):
            r = part * per + 1 + i
            stage[r % n, 0] = placed[i * CAP : (i + 1) * CAP, :HEAD]
            stage[r % n, 1] = placed[i * CAP : (i + 1) * CAP, HEAD:]
        if part == 0:
            pl.semaphore_wait(barrier, n - 1 + m - 1)
        for i in range(per):
            r = part * per + 1 + i
            if r < n:
                big[r] = pltpu.make_async_remote_copy(
                    src_ref=stage.at[r],
                    dst_ref=pool_ref.at[:, pl.ds(pl.multiple_of(g * CAP, CAP), CAP), :],
                    send_sem=big_s.at[r],
                    recv_sem=big_r.at[r],
                    device_id=(lax.rem(g + r, n), t),
                    device_id_type=MESH,
                )
                big[r].start()
    mine = pltpu.make_async_copy(
        stage.at[0], pool_ref.at[:, pl.ds(pl.multiple_of(g * CAP, CAP), CAP), :], own_sem
    )
    mine.start()
    for copy in values:
        copy.start()
    weight.start()

    for i in (3, 4, 5):
        small[i].wait()
    for h in range(GROUP):
        qf[pl.ds(h, ROWS, stride=GROUP), :] = qin[:, h * HEAD : (h + 1) * HEAD].astype(F32)
    qb[...] = qf[...].astype(BF16)
    fresh = lax.dot_general(qb[...], xb[:, :HEAD], NT, preferred_element_type=F32)
    seq_of = lax.broadcasted_iota(jnp.int32, (ROWS * GROUP, HEAD), 0) // GROUP
    for c in range(blocks):
        line = jnp.broadcast_to(rowb[c : c + 1, :], (ROWS * GROUP, HEAD))
        sf[:, c * HEAD : (c + 1) * HEAD] = jnp.where(line == seq_of, fresh[:, c * HEAD : (c + 1) * HEAD], NEG)

    pair = 2 * GROUP
    half = lax.broadcasted_iota(jnp.int32, (pair, 2 * HEAD), 0) // GROUP
    side = lax.broadcasted_iota(jnp.int32, (pair, 2 * HEAD), 1) // HEAD
    diagonal = half == side
    position = lax.broadcasted_iota(jnp.int32, (pair, SEQ), 1)
    upper_half = lax.broadcasted_iota(jnp.int32, (pair, SEQ), 0) < GROUP
    lane = lax.broadcasted_iota(jnp.int32, (GROUP, HEAD), 1)

    def score(c):
        for b in range(c * BATCH, (c + 1) * BATCH, 2):
            q = qb[pl.ds(b * GROUP, pair), :]
            q = jnp.where(diagonal, jnp.concatenate([q, q], axis=1), jnp.bfloat16(0))
            k = jnp.concatenate([kb[b], kb[b + 1]], axis=1)
            s = lax.dot_general(q, k, NT, preferred_element_type=F32)
            limit = jnp.where(upper_half, lens[b] - g * SEQ, lens[b + 1] - g * SEQ)
            sc[pl.ds(b * GROUP, pair), :] = jnp.where(position < limit, s, NEG)

    def weigh(c, held):
        for b in range(c * BATCH, (c + 1) * BATCH, 2):
            s = sc[pl.ds(b * GROUP, pair), :]
            f = sf[pl.ds(b * GROUP, pair), :]
            high = jnp.max(jnp.maximum(s, f), axis=1, keepdims=True)
            high = jnp.maximum(high, FLOOR)
            ps = jnp.exp2((s - high) * scale)
            pfr = jnp.exp2((f - high) * scale)
            total = jnp.sum(ps + pfr, axis=1, keepdims=True)
            pc[pl.ds(b * GROUP, pair), :] = ps.astype(BF16)
            pf[pl.ds(b * GROUP, pair), :] = pfr.astype(BF16)
            for j in range(2):
                rows = slice(j * GROUP, (j + 1) * GROUP)
                held = jnp.where(lane == b + j, high[rows], held)
                held = jnp.where(lane == ROWS + b + j, total[rows], held)
        return held

    def add_up(c):
        for b in range(c * BATCH, (c + 1) * BATCH, 2):
            v = jnp.concatenate([vb[b], vb[b + 1]], axis=1)
            o = lax.dot_general(pc[pl.ds(b * GROUP, pair), :], v, NN, preferred_element_type=F32)
            acc[pl.ds(b * GROUP, GROUP), :] = o[:GROUP, :HEAD]
            acc[pl.ds(b * GROUP + GROUP, GROUP), :] = o[GROUP:, HEAD:]

    held = jnp.zeros((GROUP, HEAD), F32)
    for c in range(steps + 1):
        if c < steps:
            keys[c].wait()
            score(c)
        if c >= 1:
            held = weigh(c - 1, held)

    stats[g] = held
    sent = []
    for r in range(1, n):
        copy = pltpu.make_async_remote_copy(
            src_ref=stats.at[g],
            dst_ref=stats.at[g],
            send_sem=st_s.at[r],
            recv_sem=st_r.at[r],
            device_id=(lax.rem(g + r, n), t),
            device_id_type=MESH,
        )
        copy.start()
        sent.append(copy)
    accf[...] = lax.dot_general(pf[...], xb[:, HEAD:], NN, preferred_element_type=F32)
    for c in range(steps):
        values[c].wait()
        add_up(c)

    for copy in sent:
        copy.wait_recv()
    every = [stats[i] for i in range(n)]
    top = functools.reduce(jnp.maximum, every)
    whole = jnp.zeros((GROUP, HEAD), F32)
    for one in every:
        whole = whole + jnp.exp2((one - top) * scale) * pltpu.roll(one, HEAD - ROWS, 1)
    factor = jnp.exp2((held - top) * scale) / whole
    for b in range(ROWS):
        rows = pl.ds(b * GROUP, GROUP)
        acc[rows, :] = (acc[rows, :] + accf[rows, :]) * factor[:, b : b + 1]
    rs_out[...] = acc[...].astype(BF16).reshape(n, chunk, HEAD)
    rs_in[g] = rs_out[g]
    shared = []
    for r in range(1, n):
        d = lax.rem(g + r, n)
        copy = pltpu.make_async_remote_copy(
            src_ref=rs_out.at[d],
            dst_ref=rs_in.at[g],
            send_sem=rs_s.at[r],
            recv_sem=rs_r.at[r],
            device_id=(d, t),
            device_id_type=MESH,
        )
        copy.start()
        shared.append(copy)
    for copy in shared:
        copy.wait_recv()
    attended = rs_in[0].astype(F32)
    for i in range(1, n):
        attended = attended + rs_in[i].astype(F32)
    ag[g] = attended.astype(BF16)
    gathered = []
    for r in range(1, n):
        copy = pltpu.make_async_remote_copy(
            src_ref=ag.at[g],
            dst_ref=ag.at[g],
            send_sem=ag_s.at[r],
            recv_sem=ag_r.at[r],
            device_id=(lax.rem(g + r, n), t),
            device_id_type=MESH,
        )
        copy.start()
        gathered.append(copy)
    weight.wait()
    for copy in gathered:
        copy.wait_recv()

    qf[...] = ag[...].reshape(ROWS * GROUP, HEAD).astype(F32)
    heads = [qf[pl.ds(h, ROWS, stride=GROUP), :].astype(BF16) for h in range(GROUP)]
    term = lax.dot_general(jnp.concatenate(heads, axis=1), wb[...], NN, preferred_element_type=F32)
    low = lax.broadcasted_iota(jnp.int32, (ROWS // 2, HEAD), 1) < HEAD // 2
    for j in range(m // 2):
        first = term[: ROWS // 2, j * HEAD : (j + 1) * HEAD]
        second = term[ROWS // 2 :, j * HEAD : (j + 1) * HEAD]
        tp_out[2 * j] = jnp.where(low, first, pltpu.roll(second, HEAD // 2, 1)).astype(BF16)
        tp_out[2 * j + 1] = jnp.where(low, pltpu.roll(first, HEAD // 2, 1), second).astype(BF16)
    tp_in[t] = tp_out[t]
    terms = []
    for r in range(1, m):
        d = lax.rem(t + r, m)
        copy = pltpu.make_async_remote_copy(
            src_ref=tp_out.at[d],
            dst_ref=tp_in.at[t],
            send_sem=tp_s.at[r],
            recv_sem=tp_r.at[r],
            device_id=(g, d),
            device_id_type=MESH,
        )
        copy.start()
        terms.append(copy)
    for copy in terms:
        copy.wait_recv()
    mixed = tp_in[0].astype(F32)
    for i in range(1, m):
        mixed = mixed + tp_in[i].astype(F32)
    mixed_ref[: ROWS // 2, :] = mixed[:, : HEAD // 2].astype(BF16)
    mixed_ref[ROWS // 2 :, :] = pltpu.roll(mixed, HEAD // 2, 1)[:, : HEAD // 2].astype(BF16)

    for copy in sent + shared + gathered + terms + big[1:]:
        copy.wait_send()
    mine.wait()
    for copy in big[1:]:
        copy.wait_recv()


def on_device(n, m, queries, cache_keys, cache_values, lengths, new_keys, new_values, new_rows, owners, out_weight):
    any_space = pl.BlockSpec(memory_space=pl.ANY)
    dma = pltpu.SemaphoreType.DMA
    steps = ROWS // BATCH
    return pl.pallas_call(
        functools.partial(kernel, n, m),
        out_shape=(
            jax.ShapeDtypeStruct((ROWS, HEAD // 2), BF16),
            jax.ShapeDtypeStruct((2, n * CAP, HEAD), BF16),
        ),
        in_specs=[any_space] * 9,
        out_specs=(pl.BlockSpec(memory_space=pltpu.VMEM), any_space),
        scratch_shapes=[
            pltpu.VMEM((ROWS, SEQ, HEAD), BF16),
            pltpu.VMEM((ROWS, SEQ, HEAD), BF16),
            pltpu.VMEM((FRESH, 2 * HEAD), BF16),
            pltpu.VMEM(out_weight.shape, BF16),
            pltpu.VMEM((ROWS, GROUP * HEAD), BF16),
            pltpu.VMEM((ROWS * GROUP, HEAD), F32),
            pltpu.VMEM((ROWS * GROUP, HEAD), BF16),
            pltpu.SMEM((ROWS,), jnp.int32),
            pltpu.VMEM((FRESH // HEAD, HEAD), jnp.int32),
            pltpu.VMEM((FRESH // HEAD, HEAD), jnp.int32),
            pltpu.VMEM((n, 2, CAP, HEAD), BF16),
            pltpu.VMEM((ROWS * GROUP, SEQ), F32),
            pltpu.VMEM((ROWS * GROUP, FRESH), F32),
            pltpu.VMEM((ROWS * GROUP, SEQ), BF16),
            pltpu.VMEM((ROWS * GROUP, FRESH), BF16),
            pltpu.VMEM((ROWS * GROUP, HEAD), F32),
            pltpu.VMEM((ROWS * GROUP, HEAD), F32),
            pltpu.VMEM((n, GROUP, HEAD), F32),
            pltpu.VMEM((n, ROWS * GROUP // n, HEAD), BF16),
            pltpu.VMEM((n, ROWS * GROUP // n, HEAD), BF16),
            pltpu.VMEM((n, ROWS * GROUP // n, HEAD), BF16),
            pltpu.VMEM((m, ROWS // 2, HEAD), BF16),
            pltpu.VMEM((m, ROWS // 2, HEAD), BF16),
            dma((7,)),
            dma((steps,)),
            dma((steps,)),
            dma,
        ]
        + [dma((n,))] * 8
        + [dma((m,))] * 2,
        compiler_params=pltpu.CompilerParams(
            collective_id=0, has_side_effects=True, vmem_limit_bytes=60 << 20
        ),
        name="decode",
    )(
        queries,
        cache_keys,
        cache_values,
        lengths,
        new_keys,
        new_values,
        new_rows.reshape(FRESH // HEAD, HEAD),
        owners.reshape(FRESH // HEAD, HEAD),
        out_weight,
    )


def solution(mesh):
    placed = (
        P(None, "tp"),
        P(None, "grp", "tp"),
        P(None, "grp", "tp"),
        P(),
        P("grp", "tp"),
        P("grp", "tp"),
        P("grp"),
        P("grp", None),
        P("tp", "grp"),
    )
    return jax.shard_map(
        functools.partial(on_device, mesh.shape["grp"], mesh.shape["tp"]),
        mesh=mesh,
        in_specs=placed,
        out_specs=(P(None, ("grp", "tp")), P(None, "grp", "tp")),
        check_vma=False,
    )
```

time: 170 us -> 46.6 us (0.27); the launches traced: 167 us -> 46.4 us
  waiting for transfers between devices: 49.8 us -> 0 us
  Pallas kernels: 0 us -> 42.2 us
  blocking collectives: 34.2 us -> 0 us
  other arithmetic: 29.2 us -> 0 us
  matrix products: 20.1 us -> 0 us
  between operations: 14.2 us -> 0.64 us
  starting transfers between devices: 12.8 us -> 0 us
  local copies, waits for them, and re-layouts: 6.42 us -> 3.56 us
    pallas_call x0 -> x1, Pallas kernels: none -> 42.2 us  [on_device(): pl.pallas_call(functools.partial(kernel, n, m), out_shape=(jax.ShapeDtype...]
    all_gather x2 -> x0, blocking collectives: 34.2 us -> none  [combined_all(): gathered = jax.tree.map(lambda a: lax.all_gather(a, axis), part)]
    unnamed x3 -> x0, waiting for transfers between devices: 29.3 us -> none
    dot_general x5 -> x0, matrix products: 18.9 us -> none  [the longest x2 8.95 us: finish_partial(): jnp.einsum(form, weights, values.astype(jnp.float32), precision=lax.Preci...]
    add x18 -> x0, other arithmetic: 16.7 us -> none  [the longest x15 16 us: join_partials(): summed_a * factor_a[..., None] + summed_b * factor_b[..., None]]
    all_to_all x2 -> x0, starting transfers between devices: 12.7 us -> none  [the longest x1 8.6 us: on_device(): lax.all_to_all(outgoing_rows, 'grp', split_axis=0, concat_axis=0, tiled=T...]
    all_to_all x2 -> x0, waiting for transfers between devices: 11.9 us -> none  [the longest x1 9.18 us: on_device(): lax.all_to_all(outgoing, 'grp', split_axis=0, concat_axis=0, tiled=True)]
    all_gather x1 -> x0, waiting for transfers between devices: 8.61 us -> none  [combined_all(): gathered = jax.tree.map(lambda a: lax.all_gather(a, axis), part)]
  transfers between devices with their start and end apart: 4 -> 0, of which waited for: 4 -> 0; matrix products, arithmetic and copies ran while one was open for 7% -> 0% of each run, Pallas kernels for 0% -> 0%
where the time goes in v1:
time: 46.6 us; the launch traced here: 46.4 us
  Pallas kernels  42.2 us (91%)
  local copies, waits for them, and re-layouts  3.56 us (8%)
  between operations  0.64 us (1%)
    pallas_call x1, Pallas kernels, on_device(): pl.pallas_call(functools.partial(kernel, n, m), out_shape=(jax.ShapeDtype...  42.2 us
    unnamed x2, local copies, waits for them, and re-layouts  3.56 us

profile of v1, /device:TPU:1, one launch (start us, length us, event | category | flops | bytes accessed | tf_op | source)
XLA Modules:
  0.0 46.4 jit_solution(18053006970350254968)
XLA Ops:
  0.6 42.2 %decode.1 = (bf16[32,64]{1,0:T(8,128)(2,1)}, bf16[2,2048,128]{2,1,0:T(8,128)(2,1)}) custom-call(bf16[32,1024]{1,0:T(8,128)(2,1)} %q_hbm.1, bf16[32,1024,128]{2,1,0:T(8,128)(2,1)} %ck_hbm.1, bf16[32,1024,128]{2,1,0:T(8,128)(2,1)} %cv_hbm.1, s32[32]{0:T(128)} %len_hbm.1, bf16[1024,128]{1,0:T(8,128)(2,1)} %nk_hbm.1, bf16[1024,128]{1,0:T(8,128)(2,1)} %nv_hbm.1, ...), custom_call_target="tpu_custom_call" | custom-call | tf_op jit(solution)/shard_map/decode/pallas_call | solution.py:298
  42.8 1.3 %copy.13 = bf16[32,64]{1,0:T(8,128)(2,1)} copy(bf16[32,64]{1,0:T(8,128)(2,1)} %get-tuple-element.4) | data formatting | bytes 8192
  44.1 2.3 %copy.14 = bf16[2,2048,128]{2,1,0:T(8,128)(2,1)} copy(bf16[2,2048,128]{2,1,0:T(8,128)(2,1)} %get-tuple-element.5) | data formatting | bytes 2097152

commit v2 on v1

v2 whole, which is shorter than its diff:
```python
import functools
import math

import jax
import jax.numpy as jnp
from jax import lax
from jax.experimental import pallas as pl
from jax.experimental.pallas import tpu as pltpu
from jax.sharding import PartitionSpec as P

MESH = pl.DeviceIdType.MESH
NT = (((1,), (1,)), ((), ()))
NN = (((1,), (0,)), ((), ()))
NEG = -1.0e30
FLOOR = -1.0e20
ROWS = 32
GROUP = 8
HEAD = 128
SEQ = 1024
FRESH = 1024
CAP = 128
BATCH = 4
SIDE = 4
PIECES = 4
AHEAD, GREET, FIRST, MIDDLE, LATE = 2, -1, 5, 10, 13
ORDER = tuple(sorted(((a, b) for a in range(SIDE) for b in range(SIDE)), key=lambda o: (-(2 - abs(2 - o[0])) - (2 - abs(2 - o[1])), o)))
F32 = jnp.float32
BF16 = jnp.bfloat16


def kernel(
    n,
    m,
    q_hbm, ck_hbm, cv_hbm, len_hbm, nk_hbm, nv_hbm, rows_hbm, own_hbm, w_hbm,
    mixed_ref, pool_ref,
    kb, vb, xb, wb, qin, qf, qb, lens, rowb, ownb,
    stage, sc, sf, pc, pf, accf, rs_out, rs_in, ag, core_out, core_in, x_out, x_in,
    in_sem, k_sem, v_sem, own_sem, big_s, big_r, rs_s, rs_r, ag_s, ag_r, x_s, x_r,
):
    g = lax.axis_index("grp")
    t = lax.axis_index("tp")
    y, z = g // SIDE, lax.rem(g, SIDE)
    x, core = t // 2, lax.rem(t, 2)
    mine = lax.rem(z + 2 * y, SIDE)
    scale = (HEAD**-0.5) * math.log2(math.e)
    steps = ROWS // BATCH
    part_rows = ROWS // SIDE
    blocks = FRESH // HEAD

    small = [
        pltpu.make_async_copy(own_hbm, ownb, in_sem.at[0]),
        pltpu.make_async_copy(nk_hbm, xb.at[:, pl.ds(0, HEAD)], in_sem.at[1]),
        pltpu.make_async_copy(nv_hbm, xb.at[:, pl.ds(HEAD, HEAD)], in_sem.at[2]),
        pltpu.make_async_copy(q_hbm, qin, in_sem.at[3]),
        pltpu.make_async_copy(rows_hbm, rowb, in_sem.at[4]),
        pltpu.make_async_copy(len_hbm, lens, in_sem.at[5]),
    ]
    weight = pltpu.make_async_copy(w_hbm, wb, in_sem.at[6])
    keys = [
        pltpu.make_async_copy(ck_hbm.at[pl.ds(c * BATCH, BATCH)], kb.at[pl.ds(c * BATCH, BATCH)], k_sem.at[c])
        for c in range(steps)
    ]
    values = [
        pltpu.make_async_copy(cv_hbm.at[pl.ds(c * BATCH, BATCH)], vb.at[pl.ds(c * BATCH, BATCH)], v_sem.at[c])
        for c in range(steps)
    ]
    for copy in small + keys:
        copy.start()

    barrier = pltpu.get_barrier_semaphore()
    for r in range(1, n):
        pl.semaphore_signal(barrier, inc=1, device_id=(lax.rem(g + r, n), t), device_id_type=MESH)
    pl.semaphore_signal(barrier, inc=1, device_id=(g, 2 * x + 1 - core), device_id_type=MESH)
    for r in range(1, SIDE):
        pl.semaphore_signal(
            barrier, inc=1, device_id=(g, 2 * lax.rem(x + r, SIDE) + core), device_id_type=MESH
        )

    small[0].wait()
    own = ownb[...]
    hot = jnp.concatenate([(own == o).astype(F32) for o in range(n)], axis=0).astype(BF16)
    ri = lax.broadcasted_iota(jnp.int32, (HEAD, HEAD), 0)
    ci = lax.broadcasted_iota(jnp.int32, (HEAD, HEAD), 1)
    before = (ri < ci).astype(F32).astype(BF16)
    ra = lax.broadcasted_iota(jnp.int32, (n * blocks, n * blocks), 0)
    ca = lax.broadcasted_iota(jnp.int32, (n * blocks, n * blocks), 1)
    upper = jnp.logical_and(ra // blocks == ca // blocks, ca < ra).astype(F32).astype(BF16)
    within = lax.dot_general(hot, before, NN, preferred_element_type=F32)
    ahead = lax.dot_general(upper, hot, NN, preferred_element_type=F32).astype(BF16)
    ahead = lax.dot_general(ahead, jnp.ones((HEAD, HEAD), BF16), NN, preferred_element_type=F32)
    counted = (within + ahead) * hot.astype(F32)
    rank = counted[0:blocks]
    for o in range(1, n):
        rank = rank + counted[o * blocks : (o + 1) * blocks]

    slot = lax.broadcasted_iota(jnp.int32, (CAP, HEAD), 0).astype(F32).astype(BF16)

    def toward(r):
        dy, dz = ORDER[r - 1]
        return lax.rem(y + dy, SIDE) * SIDE + lax.rem(z + dz, SIDE)

    big = [
        pltpu.make_async_remote_copy(
            src_ref=stage.at[r],
            dst_ref=pool_ref.at[:, pl.ds(pl.multiple_of(g * CAP, CAP), CAP), :],
            send_sem=big_s.at[r],
            recv_sem=big_r.at[r],
            device_id=(toward(r), t),
            device_id_type=MESH,
        )
        for r in range(1, n)
    ]
    own_part = pltpu.make_async_copy(
        stage.at[0], pool_ref.at[:, pl.ds(pl.multiple_of(g * CAP, CAP), CAP), :], own_sem
    )
    per = 4

    def place(part):
        lhs = []
        for r in range(part * per + 1, part * per + per + 1):
            d = toward(r)
            named = jnp.where(own == d, rank, -1.0)
            columns = []
            for c in range(blocks):
                line = jnp.broadcast_to(named[c : c + 1, :], (CAP, HEAD)).astype(BF16)
                columns.append(jnp.where(line == slot, jnp.bfloat16(1), jnp.bfloat16(0)))
            lhs.append(jnp.concatenate(columns, axis=1))
        placed = lax.dot_general(
            jnp.concatenate(lhs, axis=0), xb[...], NN, preferred_element_type=F32
        ).astype(BF16)
        for i in range(per):
            r = part * per + 1 + i
            stage[r % n, 0] = placed[i * CAP : (i + 1) * CAP, :HEAD]
            stage[r % n, 1] = placed[i * CAP : (i + 1) * CAP, HEAD:]

    def send(first, last):
        for r in range(first, last + 1):
            big[r - 1].start()

    small[1].wait()
    small[2].wait()
    for part in range(AHEAD):
        place(part)
    if GREET < 0:
        pl.semaphore_wait(barrier, n - 1 + SIDE)
        send(1, FIRST)

    for i in (3, 4, 5):
        small[i].wait()
    for h in range(GROUP):
        qf[pl.ds(h, ROWS, stride=GROUP), :] = qin[:, h * HEAD : (h + 1) * HEAD].astype(F32)
    qb[...] = qf[...].astype(BF16)
    fresh = lax.dot_general(qb[...], xb[:, :HEAD], NT, preferred_element_type=F32)
    seq_of = lax.broadcasted_iota(jnp.int32, (ROWS * GROUP, HEAD), 0) // GROUP
    for c in range(blocks):
        line = jnp.broadcast_to(rowb[c : c + 1, :], (ROWS * GROUP, HEAD))
        sf[:, c * HEAD : (c + 1) * HEAD] = jnp.where(line == seq_of, fresh[:, c * HEAD : (c + 1) * HEAD], NEG)

    pair = 2 * GROUP
    half = lax.broadcasted_iota(jnp.int32, (pair, 2 * HEAD), 0) // GROUP
    side = lax.broadcasted_iota(jnp.int32, (pair, 2 * HEAD), 1) // HEAD
    diagonal = half == side
    position = lax.broadcasted_iota(jnp.int32, (pair, SEQ), 1)
    upper_half = lax.broadcasted_iota(jnp.int32, (pair, SEQ), 0) < GROUP
    lane = lax.broadcasted_iota(jnp.int32, (GROUP, HEAD), 1)

    def score(c):
        for b in range(c * BATCH, (c + 1) * BATCH, 2):
            q = qb[pl.ds(b * GROUP, pair), :]
            q = jnp.where(diagonal, jnp.concatenate([q, q], axis=1), jnp.bfloat16(0))
            k = jnp.concatenate([kb[b], kb[b + 1]], axis=1)
            s = lax.dot_general(q, k, NT, preferred_element_type=F32)
            limit = jnp.where(upper_half, lens[b] - g * SEQ, lens[b + 1] - g * SEQ)
            sc[pl.ds(b * GROUP, pair), :] = jnp.where(position < limit, s, NEG)

    def weigh(c, held):
        for b in range(c * BATCH, (c + 1) * BATCH, 2):
            s = sc[pl.ds(b * GROUP, pair), :]
            f = sf[pl.ds(b * GROUP, pair), :]
            high = jnp.max(jnp.maximum(s, f), axis=1, keepdims=True)
            high = jnp.maximum(high, FLOOR).astype(BF16).astype(F32)
            ps = jnp.exp2((s - high) * scale)
            pfr = jnp.exp2((f - high) * scale)
            total = jnp.sum(ps + pfr, axis=1, keepdims=True)
            pc[pl.ds(b * GROUP, pair), :] = ps.astype(BF16)
            pf[pl.ds(b * GROUP, pair), :] = pfr.astype(BF16)
            for j in range(2):
                rows = slice(j * GROUP, (j + 1) * GROUP)
                place_of = (b + j) % part_rows
                held = jnp.where(lane == place_of, high[rows], held)
                held = jnp.where(lane == part_rows + place_of, total[rows], held)
        return held

    def add_up(c):
        for b in range(c * BATCH, (c + 1) * BATCH, 2):
            v = jnp.concatenate([vb[b], vb[b + 1]], axis=1)
            o = lax.dot_general(pc[pl.ds(b * GROUP, pair), :], v, NN, preferred_element_type=F32)
            o = jnp.concatenate([o[:GROUP, :HEAD], o[GROUP:, HEAD:]], axis=0) + accf[pl.ds(b * GROUP, pair), :]
            rs_out[b // part_rows, pl.ds((b % part_rows) * GROUP, pair), :] = o.astype(BF16)

    held = [jnp.zeros((GROUP, HEAD), F32)] * SIDE
    each = part_rows // BATCH
    for c in range(steps + 1):
        if c < steps:
            keys[c].wait()
            values[c].start()
            if c == GREET:
                pl.semaphore_wait(barrier, n - 1 + SIDE)
                send(1, FIRST)
            score(c)
        if c >= 1:
            held[(c - 1) // each] = weigh(c - 1, held[(c - 1) // each])
    for j in range(SIDE):
        coarse = held[j].astype(BF16)
        rest = (held[j] - coarse.astype(F32)).astype(BF16)
        rs_out[j, pl.ds(part_rows * GROUP, pair), :] = jnp.concatenate([coarse, rest], axis=0)
    accf[...] = lax.dot_general(pf[...], xb[:, HEAD:], NN, preferred_element_type=F32)

    weight.start()
    if GREET >= steps:
        pl.semaphore_wait(barrier, n - 1 + SIDE)
        send(1, FIRST)

    for j in range(SIDE):
        for c in range(j * each, (j + 1) * each):
            values[c].wait()
            add_up(c)
        for r in range(SIDE):
            yy = lax.rem(y + r, SIDE)
            d = yy * SIDE + lax.rem(j + 2 * yy, SIDE)
            copy = pltpu.make_async_remote_copy(
                src_ref=rs_out.at[j],
                dst_ref=rs_in.at[g],
                send_sem=rs_s.at[d],
                recv_sem=rs_r.at[g],
                device_id=(d, t),
                device_id_type=MESH,
            )
            if r == 0:
                pl.when(d != g)(copy.start)
            else:
                copy.start()
    for part in range(n // per):
        if part >= AHEAD:
            place(part)
        send(max(FIRST, part * per) + 1, min((part + 1) * per, MIDDLE))
    own_part.start()
    rs_in[g] = rs_out[mine]
    for r in range(1, n):
        i = lax.rem(g + r, n)
        pltpu.make_async_copy(rs_in.at[i], rs_in.at[i], rs_r.at[i]).wait()
    tails = [rs_in[i, pl.ds(part_rows * GROUP, pair), :].astype(F32) for i in range(n)]
    highs = [tail[:GROUP] for tail in tails]
    sums = [pltpu.roll(tail[:GROUP] + tail[GROUP:], HEAD - part_rows, 1) for tail in tails]
    top = functools.reduce(jnp.maximum, highs)
    parts = [jnp.exp2((one - top) * scale) for one in highs]
    whole = parts[0] * sums[0]
    for i in range(1, n):
        whole = whole + parts[i] * sums[i]
    inverse = 1.0 / whole
    parts = [one * inverse for one in parts]
    for b in range(0, part_rows, 2):
        rows = pl.ds(b * GROUP, pair)
        total = jnp.zeros((pair, HEAD), F32)
        for i in range(n):
            factor = jnp.concatenate(
                [jnp.broadcast_to(parts[i][:, b + j : b + j + 1], (GROUP, HEAD)) for j in range(2)], axis=0
            )
            total = total + rs_in[i, rows, :].astype(F32) * factor
        ag[mine, rows, :] = total.astype(BF16)
    gathered = []
    for k, d in enumerate(
        (
            y * SIDE + lax.rem(z + 1, SIDE),
            y * SIDE + lax.rem(z + SIDE - 1, SIDE),
            lax.rem(y + 1, SIDE) * SIDE + z,
        )
    ):
        copy = pltpu.make_async_remote_copy(
            src_ref=ag.at[mine],
            dst_ref=ag.at[mine],
            send_sem=ag_s.at[k],
            recv_sem=ag_r.at[k],
            device_id=(d, t),
            device_id_type=MESH,
        )
        copy.start()
        gathered.append(copy)
    send(MIDDLE + 1, LATE)
    weight.wait()
    for copy in gathered:
        copy.wait_recv()

    qf[...] = ag[...].reshape(ROWS * GROUP, HEAD).astype(F32)
    heads = [qf[pl.ds(h, ROWS, stride=GROUP), :].astype(BF16) for h in range(GROUP)]
    term = lax.dot_general(jnp.concatenate(heads, axis=1), wb[...], NN, preferred_element_type=F32)
    low = lax.broadcasted_iota(jnp.int32, (ROWS // 2, HEAD), 1) < HEAD // 2
    for j in range(SIDE):
        first = term[: ROWS // 2, j * HEAD : (j + 1) * HEAD]
        second = term[ROWS // 2 :, j * HEAD : (j + 1) * HEAD]
        core_out[0, j] = jnp.where(low, first, pltpu.roll(second, HEAD // 2, 1))
        core_out[1, j] = jnp.where(low, pltpu.roll(first, HEAD // 2, 1), second)
    across = pltpu.make_async_remote_copy(
        src_ref=core_out.at[1 - core],
        dst_ref=core_in,
        send_sem=x_s.at[0],
        recv_sem=x_r.at[0],
        device_id=(g, 2 * x + 1 - core),
        device_id_type=MESH,
    )
    across.start()
    across.wait_recv()
    x_out[...] = core_out[core] + core_in[...]
    terms = []
    for r in range(1, SIDE):
        d = lax.rem(x + r, SIDE)
        copy = pltpu.make_async_remote_copy(
            src_ref=x_out.at[d],
            dst_ref=x_in.at[r],
            send_sem=x_s.at[r],
            recv_sem=x_r.at[r],
            device_id=(g, 2 * d + core),
            device_id_type=MESH,
        )
        copy.start()
        terms.append(copy)
    send(LATE + 1, n - 1)
    mixed = x_out[x]
    for r in range(1, SIDE):
        terms[r - 1].wait_recv()
        mixed = mixed + x_in[r]
    mixed_ref[: ROWS // 2, :] = mixed[:, : HEAD // 2].astype(BF16)
    mixed_ref[ROWS // 2 :, :] = pltpu.roll(mixed, HEAD // 2, 1)[:, : HEAD // 2].astype(BF16)

    for r in range(1, n):
        d = lax.rem(g + r, n)
        pltpu.make_async_copy(rs_in.at[d], rs_in.at[d], rs_s.at[d]).wait()
    for copy in gathered + [across] + terms + big:
        copy.wait_send()
    own_part.wait()
    for copy in big:
        copy.wait_recv()


def finish(mixed_in, pool_in, mixed_out, pool_out, sems):
    copies = [
        pltpu.make_async_copy(mixed_in, mixed_out, sems.at[0]),
        pltpu.make_async_copy(pool_in, pool_out, sems.at[1]),
    ]
    for copy in copies:
        copy.start()
    for copy in copies:
        copy.wait()


def on_device(n, m, queries, cache_keys, cache_values, lengths, new_keys, new_values, new_rows, owners, out_weight):
    any_space = pl.BlockSpec(memory_space=pl.ANY)
    vmem_space = pl.BlockSpec(memory_space=pltpu.VMEM)
    dma = pltpu.SemaphoreType.DMA
    steps = ROWS // BATCH
    wide = ROWS * GROUP
    shapes = (
        jax.ShapeDtypeStruct((ROWS, HEAD // 2), BF16),
        jax.ShapeDtypeStruct((2, n * CAP, HEAD), BF16),
    )
    made = pl.pallas_call(
        functools.partial(kernel, n, m),
        out_shape=tuple(pltpu.VMEM(shape.shape, shape.dtype) for shape in shapes),
        in_specs=[any_space] * 9,
        out_specs=(vmem_space, vmem_space),
        scratch_shapes=[
            pltpu.VMEM((ROWS, SEQ, HEAD), BF16),
            pltpu.VMEM((ROWS, SEQ, HEAD), BF16),
            pltpu.VMEM((FRESH, 2 * HEAD), BF16),
            pltpu.VMEM(out_weight.shape, BF16),
            pltpu.VMEM((ROWS, GROUP * HEAD), BF16),
            pltpu.VMEM((wide, HEAD), F32),
            pltpu.VMEM((wide, HEAD), BF16),
            pltpu.SMEM((ROWS,), jnp.int32),
            pltpu.VMEM((FRESH // HEAD, HEAD), jnp.int32),
            pltpu.VMEM((FRESH // HEAD, HEAD), jnp.int32),
            pltpu.VMEM((n, 2, CAP, HEAD), BF16),
            pltpu.VMEM((wide, SEQ), F32),
            pltpu.VMEM((wide, FRESH), F32),
            pltpu.VMEM((wide, SEQ), BF16),
            pltpu.VMEM((wide, FRESH), BF16),
            pltpu.VMEM((wide, HEAD), F32),
            pltpu.VMEM((SIDE, wide // SIDE + 2 * GROUP, HEAD), BF16),
            pltpu.VMEM((n, wide // SIDE + 2 * GROUP, HEAD), BF16),
            pltpu.VMEM((SIDE, wide // SIDE, HEAD), BF16),
            pltpu.VMEM((2, SIDE, ROWS // 2, HEAD), F32),
            pltpu.VMEM((SIDE, ROWS // 2, HEAD), F32),
            pltpu.VMEM((SIDE, ROWS // 2, HEAD), F32),
            pltpu.VMEM((SIDE, ROWS // 2, HEAD), F32),
            dma((7,)),
            dma((steps,)),
            dma((steps,)),
            dma,
        ]
        + [dma((n,))] * 4
        + [dma((SIDE,))] * 4,
        compiler_params=pltpu.CompilerParams(
            collective_id=0, has_side_effects=True, vmem_limit_bytes=60 << 20
        ),
        name="decode",
    )(
        queries,
        cache_keys,
        cache_values,
        lengths,
        new_keys,
        new_values,
        new_rows.reshape(FRESH // HEAD, HEAD),
        owners.reshape(FRESH // HEAD, HEAD),
        out_weight,
    )
    return pl.pallas_call(
        finish,
        out_shape=shapes,
        in_specs=[vmem_space] * 2,
        out_specs=(any_space, any_space),
        scratch_shapes=[dma((2,))],
        compiler_params=pltpu.CompilerParams(vmem_limit_bytes=60 << 20),
        name="finish",
    )(*(pltpu.with_memory_space_constraint(one, pltpu.VMEM) for one in made))


def solution(mesh):
    placed = (
        P(None, "tp"),
        P(None, "grp", "tp"),
        P(None, "grp", "tp"),
        P(),
        P("grp", "tp"),
        P("grp", "tp"),
        P("grp"),
        P("grp", None),
        P("tp", "grp"),
    )
    return jax.shard_map(
        functools.partial(on_device, mesh.shape["grp"], mesh.shape["tp"]),
        mesh=mesh,
        in_specs=placed,
        out_specs=(P(None, ("grp", "tp")), P(None, "grp", "tp")),
        check_vma=False,
    )
```

time: 46.6 us -> 34.9 us (0.75)
  Pallas kernels: 42.2 us -> 34.1 us
  local copies, waits for them, and re-layouts: 3.56 us -> 0 us
    pallas_call x1 -> x2, Pallas kernels: 42.2 us -> 34.1 us  [the longest x1 33.1 us: on_device(): pl.pallas_call(functools.partial(kernel, n, m), out_shape=tuple((pltpu.VM...]
    unnamed x2 -> x0, local copies, waits for them, and re-layouts: 3.56 us -> none
where the time goes in v2:
time: 34.9 us; the launch traced here: 34.8 us
  Pallas kernels  34.1 us (98%)
  between operations  0.64 us (2%)
    pallas_call x1, Pallas kernels, on_device(): pl.pallas_call(functools.partial(kernel, n, m), out_shape=tuple((pltpu.VM...  33.1 us
    pallas_call x1, Pallas kernels, on_device(): pl.pallas_call(finish, out_shape=shapes, in_specs=[vmem_space] * 2, out_s...  0.99 us

profile of v2, /device:TPU:1, one launch (start us, length us, event | category | flops | bytes accessed | tf_op | source)
XLA Modules:
  0.0 34.8 jit_solution(8068918515889638981)
XLA Ops:
  0.6 33.1 %decode.1 = (bf16[32,64]{1,0:T(8,128)(2,1)S(1)}, bf16[2,2048,128]{2,1,0:T(8,128)(2,1)S(1)}) custom-call(bf16[32,1024]{1,0:T(8,128)(2,1)} %q_hbm.1, bf16[32,1024,128]{2,1,0:T(8,128)(2,1)} %ck_hbm.1, bf16[32,1024,128]{2,1,0:T(8,128)(2,1)} %cv_hbm.1, s32[32]{0:T(128)} %len_hbm.1, bf16[1024,128]{1,0:T(8,128)(2,1)} %nk_hbm.1, bf16[1024,128]{1,0:T(8,128)(2,1)} %nv_hbm.1, ...), custom_call_target="tpu_custom_call" | custom-call | tf_op jit(solution)/shard_map/decode/pallas_call | solution.py:366
  33.8 1.0 %finish.1 = (bf16[32,64]{1,0:T(8,128)(2,1)}, bf16[2,2048,128]{2,1,0:T(8,128)(2,1)}) custom-call(bf16[32,64]{1,0:T(8,128)(2,1)S(1)} %get-tuple-element.4.mixed_in, bf16[2,2048,128]{2,1,0:T(8,128)(2,1)S(1)} %get-tuple-element.5.pool_in), custom_call_target="tpu_custom_call" | custom-call | tf_op jit(solution)/shard_map/finish/pallas_call | solution.py:417

commit v3 on v2

--- a/solution.py
+++ b/solution.py
@@ -22,7 +22,8 @@
 BATCH = 4
 SIDE = 4
 PIECES = 4
-AHEAD, GREET, FIRST, MIDDLE, LATE = 2, -1, 5, 10, 13
+PLACES = ((1, 6), (7, 10), (11, 13), (14, 16))
+AHEAD, GREET, FIRST, MIDDLE, LATE, LAST = 2, -1, 5, 6, 8, 13
 ORDER = tuple(sorted(((a, b) for a in range(SIDE) for b in range(SIDE)), key=lambda o: (-(2 - abs(2 - o[0])) - (2 - abs(2 - o[1])), o)))
 F32 = jnp.float32
 BF16 = jnp.bfloat16
@@ -113,11 +114,10 @@
     own_part = pltpu.make_async_copy(
         stage.at[0], pool_ref.at[:, pl.ds(pl.multiple_of(g * CAP, CAP), CAP), :], own_sem
     )
-    per = 4
-
     def place(part):
+        first, last = PLACES[part]
         lhs = []
-        for r in range(part * per + 1, part * per + per + 1):
+        for r in range(first, last + 1):
             d = toward(r)
             named = jnp.where(own == d, rank, -1.0)
             columns = []
@@ -128,8 +128,7 @@
         placed = lax.dot_general(
             jnp.concatenate(lhs, axis=0), xb[...], NN, preferred_element_type=F32
         ).astype(BF16)
-        for i in range(per):
-            r = part * per + 1 + i
+        for i, r in enumerate(range(first, last + 1)):
             stage[r % n, 0] = placed[i * CAP : (i + 1) * CAP, :HEAD]
             stage[r % n, 1] = placed[i * CAP : (i + 1) * CAP, HEAD:]
 
@@ -139,8 +138,7 @@
 
     small[1].wait()
     small[2].wait()
-    for part in range(AHEAD):
-        place(part)
+    place(0)
     if GREET < 0:
         pl.semaphore_wait(barrier, n - 1 + SIDE)
         send(1, FIRST)
@@ -240,10 +238,9 @@
                 pl.when(d != g)(copy.start)
             else:
                 copy.start()
-    for part in range(n // per):
-        if part >= AHEAD:
-            place(part)
-        send(max(FIRST, part * per) + 1, min((part + 1) * per, MIDDLE))
+    send(FIRST + 1, MIDDLE)
+    for part in range(1, len(PLACES)):
+        place(part)
     own_part.start()
     rs_in[g] = rs_out[mine]
     for r in range(1, n):
@@ -291,6 +288,8 @@
     for copy in gathered:
         copy.wait_recv()
 
+    send(LATE + 1, LAST)
+
     qf[...] = ag[...].reshape(ROWS * GROUP, HEAD).astype(F32)
     heads = [qf[pl.ds(h, ROWS, stride=GROUP), :].astype(BF16) for h in range(GROUP)]
     term = lax.dot_general(jnp.concatenate(heads, axis=1), wb[...], NN, preferred_element_type=F32)
@@ -324,7 +323,7 @@
         )
         copy.start()
         terms.append(copy)
-    send(LATE + 1, n - 1)
+    send(LAST + 1, n - 1)
     mixed = x_out[x]
     for r in range(1, SIDE):
         terms[r - 1].wait_recv()

time: 34.9 us -> 33.4 us (0.957)
  Pallas kernels: 34.1 us -> 32.6 us
    pallas_call x1, Pallas kernels: 33.1 us -> 31.6 us  [on_device(): pl.pallas_call(functools.partial(kernel, n, m), out_shape=tuple((pltpu.VM...]
where the time goes in v3:
time: 33.4 us; the launch traced here: 33.3 us
  Pallas kernels  32.6 us (98%)
  between operations  0.64 us (2%)
    pallas_call x1, Pallas kernels, on_device(): pl.pallas_call(functools.partial(kernel, n, m), out_shape=tuple((pltpu.VM...  31.6 us
    pallas_call x1, Pallas kernels, on_device(): pl.pallas_call(finish, out_shape=shapes, in_specs=[vmem_space] * 2, out_s...  0.99 us

profile of v3, /device:TPU:1, one launch (start us, length us, event | category | flops | bytes accessed | tf_op | source)
XLA Modules:
  0.0 33.3 jit_solution(3770722105306536563)
XLA Ops:
  0.6 31.6 %decode.1 = (bf16[32,64]{1,0:T(8,128)(2,1)S(1)}, bf16[2,2048,128]{2,1,0:T(8,128)(2,1)S(1)}) custom-call(bf16[32,1024]{1,0:T(8,128)(2,1)} %q_hbm.1, bf16[32,1024,128]{2,1,0:T(8,128)(2,1)} %ck_hbm.1, bf16[32,1024,128]{2,1,0:T(8,128)(2,1)} %cv_hbm.1, s32[32]{0:T(128)} %len_hbm.1, bf16[1024,128]{1,0:T(8,128)(2,1)} %nk_hbm.1, bf16[1024,128]{1,0:T(8,128)(2,1)} %nv_hbm.1, ...), custom_call_target="tpu_custom_call" | custom-call | tf_op jit(solution)/shard_map/decode/pallas_call | solution.py:365
  32.3 1.0 %finish.1 = (bf16[32,64]{1,0:T(8,128)(2,1)}, bf16[2,2048,128]{2,1,0:T(8,128)(2,1)}) custom-call(bf16[32,64]{1,0:T(8,128)(2,1)S(1)} %get-tuple-element.4.mixed_in, bf16[2,2048,128]{2,1,0:T(8,128)(2,1)S(1)} %get-tuple-element.5.pool_in), custom_call_target="tpu_custom_call" | custom-call | tf_op jit(solution)/shard_map/finish/pallas_call | solution.py:416

commit v4 on v3

--- a/solution.py
+++ b/solution.py
@@ -23,7 +23,7 @@
 SIDE = 4
 PIECES = 4
 PLACES = ((1, 6), (7, 10), (11, 13), (14, 16))
-AHEAD, GREET, FIRST, MIDDLE, LATE, LAST = 2, -1, 5, 6, 8, 13
+FIRST, MIDDLE, LATE, LAST = 4, 4, 5, 13
 ORDER = tuple(sorted(((a, b) for a in range(SIDE) for b in range(SIDE)), key=lambda o: (-(2 - abs(2 - o[0])) - (2 - abs(2 - o[1])), o)))
 F32 = jnp.float32
 BF16 = jnp.bfloat16
@@ -139,9 +139,8 @@
     small[1].wait()
     small[2].wait()
     place(0)
-    if GREET < 0:
-        pl.semaphore_wait(barrier, n - 1 + SIDE)
-        send(1, FIRST)
+    pl.semaphore_wait(barrier, n - 1 + SIDE)
+    send(1, FIRST)
 
     for i in (3, 4, 5):
         small[i].wait()
@@ -202,9 +201,6 @@
         if c < steps:
             keys[c].wait()
             values[c].start()
-            if c == GREET:
-                pl.semaphore_wait(barrier, n - 1 + SIDE)
-                send(1, FIRST)
             score(c)
         if c >= 1:
             held[(c - 1) // each] = weigh(c - 1, held[(c - 1) // each])
@@ -215,10 +211,6 @@
     accf[...] = lax.dot_general(pf[...], xb[:, HEAD:], NN, preferred_element_type=F32)
 
     weight.start()
-    if GREET >= steps:
-        pl.semaphore_wait(barrier, n - 1 + SIDE)
-        send(1, FIRST)
-
     for j in range(SIDE):
         for c in range(j * each, (j + 1) * each):
             values[c].wait()
@@ -268,9 +260,9 @@
     gathered = []
     for k, d in enumerate(
         (
+            lax.rem(y + 1, SIDE) * SIDE + z,
             y * SIDE + lax.rem(z + 1, SIDE),
             y * SIDE + lax.rem(z + SIDE - 1, SIDE),
-            lax.rem(y + 1, SIDE) * SIDE + z,
         )
     ):
         copy = pltpu.make_async_remote_copy(
@@ -288,7 +280,10 @@
     for copy in gathered:
         copy.wait_recv()
 
-    send(LATE + 1, LAST)
+    for r in range(LATE + 1, n):
+        pl.when(toward(r) == 0)(big[r - 1].start)
+    for r in range(LATE + 1, LAST + 1):
+        pl.when(toward(r) != 0)(big[r - 1].start)
 
     qf[...] = ag[...].reshape(ROWS * GROUP, HEAD).astype(F32)
     heads = [qf[pl.ds(h, ROWS, stride=GROUP), :].astype(BF16) for h in range(GROUP)]
@@ -311,7 +306,7 @@
     across.wait_recv()
     x_out[...] = core_out[core] + core_in[...]
     terms = []
-    for r in range(1, SIDE):
+    for r in (2, 3, 1):
         d = lax.rem(x + r, SIDE)
         copy = pltpu.make_async_remote_copy(
             src_ref=x_out.at[d],
@@ -323,10 +318,11 @@
         )
         copy.start()
         terms.append(copy)
-    send(LAST + 1, n - 1)
+    for r in range(LAST + 1, n):
+        pl.when(toward(r) != 0)(big[r - 1].start)
     mixed = x_out[x]
     for r in range(1, SIDE):
-        terms[r - 1].wait_recv()
+        terms[(2, 3, 1).index(r)].wait_recv()
         mixed = mixed + x_in[r]
     mixed_ref[: ROWS // 2, :] = mixed[:, : HEAD // 2].astype(BF16)
     mixed_ref[ROWS // 2 :, :] = pltpu.roll(mixed, HEAD // 2, 1)[:, : HEAD // 2].astype(BF16)

time: 33.4 us -> 32.9 us (0.985)
  Pallas kernels: 32.6 us -> 32.1 us
    pallas_call x1, Pallas kernels: 31.6 us -> 31.1 us  [on_device(): pl.pallas_call(functools.partial(kernel, n, m), out_shape=tuple((pltpu.VM...]
where the time goes in v4:
time: 32.9 us; the launch traced here: 32.8 us
  Pallas kernels  32.1 us (98%)
  between operations  0.64 us (2%)
    pallas_call x1, Pallas kernels, on_device(): pl.pallas_call(functools.partial(kernel, n, m), out_shape=tuple((pltpu.VM...  31.1 us
    pallas_call x1, Pallas kernels, on_device(): pl.pallas_call(finish, out_shape=shapes, in_specs=[vmem_space] * 2, out_s...  0.99 us

profile of v4, /device:TPU:1, one launch (start us, length us, event | category | flops | bytes accessed | tf_op | source)
XLA Modules:
  0.0 32.8 jit_solution(2180638045474152088)
XLA Ops:
  0.6 31.1 %decode.1 = (bf16[32,64]{1,0:T(8,128)(2,1)S(1)}, bf16[2,2048,128]{2,1,0:T(8,128)(2,1)S(1)}) custom-call(bf16[32,1024]{1,0:T(8,128)(2,1)} %q_hbm.1, bf16[32,1024,128]{2,1,0:T(8,128)(2,1)} %ck_hbm.1, bf16[32,1024,128]{2,1,0:T(8,128)(2,1)} %cv_hbm.1, s32[32]{0:T(128)} %len_hbm.1, bf16[1024,128]{1,0:T(8,128)(2,1)} %nk_hbm.1, bf16[1024,128]{1,0:T(8,128)(2,1)} %nv_hbm.1, ...), custom_call_target="tpu_custom_call" | custom-call | tf_op jit(solution)/shard_map/decode/pallas_call | solution.py:361
  31.8 1.0 %finish.1 = (bf16[32,64]{1,0:T(8,128)(2,1)}, bf16[2,2048,128]{2,1,0:T(8,128)(2,1)}) custom-call(bf16[32,64]{1,0:T(8,128)(2,1)S(1)} %get-tuple-element.4.mixed_in, bf16[2,2048,128]{2,1,0:T(8,128)(2,1)S(1)} %get-tuple-element.5.pool_in), custom_call_target="tpu_custom_call" | custom-call | tf_op jit(solution)/shard_map/finish/pallas_call | solution.py:412
